TPU v7x, 32 devices: a whole 2x2x4 slice. The times are simulated.
32 devices in a mesh: amp: 8 (over y, x, core), slab: 4 (over z).
Axes of the slice: x: 2, y: 2, z: 4, core: 2. Of those that a mesh axis runs over, the one named last changes fastest.
Arguments:
- v_slab: bfloat16 [131072, 1024], P('amp', 'slab'), may hold values from -0.25 to 0.25
- t_amp: bfloat16 [8, 800, 1024], P(None, 'amp', 'slab'), may hold values from -6 to 6
- ab_tile_irrep: int32 [1024], replicated, may hold values from 0 to 7, as said below
Outputs:
- residual: bfloat16 [131072, 800], P(('amp', 'slab'))
Inputs may be any that keep to these rules, and one draw needn't show every extreme that they name: `ab_tile_irrep`: Non-decreasing, takes every value from 0 to 7; the 128 consecutive tiles of one index of amp hold at most two distinct values, and in every draw some indices hold two.
All inputs are finite; a program needn't handle non-finite values.
Results may differ from a plain program's by a relative error of at most 0.009.
Values may be sent and summed in bfloat16 or wider, within the bound.
A program may use at most 192 MiB of HBM per device.

v0:
```python
import jax
import jax.numpy as jnp
from jax import lax
from jax.sharding import PartitionSpec as P

TB = 128


def on_device(v_slab, t_amp, ab_tile_irrep):
    rows_local, cd_local = v_slab.shape
    tile_rows = TB
    amp_count = lax.axis_size("amp")
    slab_count = lax.axis_size("slab")
    tiles_local = rows_local // tile_rows
    layout = ab_tile_irrep.reshape(amp_count, tiles_local)
    own_irreps = lax.dynamic_index_in_dim(layout, lax.axis_index("amp"), 0, keepdims=False)
    wanted = jnp.stack([layout[:, 0], layout[:, -1]], axis=0)
    outgoing = jnp.take(t_amp, wanted, axis=0)
    incoming = lax.all_to_all(outgoing, "amp", split_axis=1, concat_axis=1, tiled=True)
    blocks_held = incoming.reshape(2, -1, cd_local)
    slot_index = (own_irreps != own_irreps[0]).astype(jnp.int32)
    row_count = lax.axis_size("slab") * (rows_local // slab_count)
    v_rows = v_slab
    v_rows = v_rows.reshape(row_count // tile_rows, tile_rows, cd_local)
    chosen = jnp.take(blocks_held, slot_index, axis=0)
    product = jnp.einsum("tkc,tjc->tkj", v_rows, chosen, preferred_element_type=jnp.float32)
    return lax.psum_scatter(
        product.reshape(row_count, -1).astype(jnp.bfloat16), "slab", scatter_dimension=0, tiled=True
    )


def solution(mesh):
    placed = (P("amp", "slab"), P(None, "amp", "slab"), P())
    return jax.shard_map(
        on_device, mesh=mesh, in_specs=placed, out_specs=P(("amp", "slab"), None), check_vma=False
    )
```

profile of v0, /device:TPU:8, one launch (start us, length us, event | category | flops | bytes accessed | tf_op | source)
XLA Modules:
  0.0 533.4 jit_solution(12849828926165120888)
XLA Ops:
  6.5 0.0 copy-start
  6.5 1.0 slice_reduce_fusion.1
  7.5 0.1 copy.6
  7.7 0.1 reshape.153
  7.7 0.0 copy-done
  7.7 2.9 gather_fusion
  10.7 1.9 broadcast_select_fusion
  12.5 3.7 all-to-all-start
  16.2 0.0 reduce-scatter.2.cloned.1.call-start
  16.3 0.7 constant_dynamic-slice_fusion
  17.0 0.7 fusion.7
  17.7 0.7 compare_and_fusion.1
  18.4 10.7 %all-to-all-done = bf16[2,8,100,256]{3,0,2,1:T(2,128)(2,1)S(1)} async-done(((bf16[2,8,100,256]{3,0,2,1:T(2,128)(2,1)}), bf16[2,8,100,256]{3,0,2,1:T(2,128)(2,1)S(1)}, u32[]{:S(2)}, u32[]{:S(2)}) %all-to-all-start) | async-done | bytes 819232 | tf_op jit(solution)/shard_map/all_to_all | solution.py:19
  29.2 0.1 copy.10
  29.3 18.5 %gather_fusion.1 = bf16[128,800,256]{2,1,0:T(8,128)(2,1)} fusion(bf16[2,800,256]{2,1,0:T(8,128)(2,1)S(1)} %copy.10, s32[1024]{0:T(1024)S(1)} %pad_clamp_fusion), kind=kCustom, calls=%fused_computation.1 | custom fusion | bytes 104858112 | tf_op jit(solution)/shard_map/jit(_take)/gather | solution.py:25
  47.8 0.0 copy-start.1
  47.8 30.6 %convert_bitcast_fusion = bf16[128,100,8,128]{3,2,1,0:T(8,128)(2,1)} fusion(bf16[128,128,256]{2,1,0:T(8,128)(2,1)} %bitcast.38, bf16[128,800,256]{2,1,0:T(8,128)(2,1)} %gather_fusion.1, pred[128]{0:T(512)(128)(4,1)S(1)} %compare_and_fusion.1), kind=kOutput, calls=%fused_computation.6 | convolution fusion | flops 6750208000 | bytes 87031936 | tf_op jit(solution)/shard_map/tkc,tjc->tkj/dot_general | solution.py:26
  78.4 17.7 %copy.14 = bf16[128,100,8,128]{3,2,0,1:T(8,128)(2,1)} copy(bf16[128,100,8,128]{3,2,1,0:T(8,128)(2,1)} %convert_bitcast_fusion) | data formatting | bytes 52428800 | tf_op jit(solution)/shard_map/convert_element_type | solution.py:28
  96.2 0.0 reduce-scatter.2.cloned.1.call-update
  96.2 430.4 %reduce-scatter.2.cloned.1.call-done = bf16[4096,800]{0,1:T(8,128)(2,1)} async-done(((bf16[16384,800]{0,1:T(8,128)(2,1)}), bf16[4096,800]{0,1:T(8,128)(2,1)}) %reduce-scatter.2.cloned.1.call-update) | async-done | bytes 6553616 | tf_op jit(solution)/shard_map/reduce_scatter | solution.py:27
  526.6 0.0 copy-done.1
  (4 shorter events, 0.1 us)
Async XLA Ops:
  6.5 1.2 copy-start
  12.5 16.7 %all-to-all-start = ((bf16[2,8,100,256]{3,0,2,1:T(2,128)(2,1)}), bf16[2,8,100,256]{3,0,2,1:T(2,128)(2,1)S(1)}, u32[]{:S(2)}, u32[]{:S(2)}) async-start(bf16[2,8,100,256]{3,0,2,1:T(2,128)(2,1)} %broadcast_select_fusion), calls=%async_computation | async-start | bytes 1638400 | tf_op jit(solution)/shard_map/all_to_all | solution.py:19
  16.2 510.4 %reduce-scatter.2.cloned.1.call-start = ((), (), s32[]{:S(2)}) async-start(), calls=%async_computation.2 | async-start | bytes 32768000 | tf_op jit(solution)/shard_map/reduce_scatter | solution.py:27
  47.8 478.8 %copy-start.1 = (bf16[8,100,256]{2,0,1:T(8,128)(2,1)S(1)}, bf16[8,100,256]{2,0,1:T(8,128)(2,1)}, u32[]{:S(2)}) copy-start(bf16[8,100,256]{2,0,1:T(8,128)(2,1)} %param.4) | copy-start | bytes 1228804
Sparse Core Ops, SparseCore 0:
  96.3 430.2 reduce-scatter.1
where the time goes:
time: 536 us; the launch traced here: 533 us
  waiting for transfers between devices  441 us (82%)
  local copies, waits for them, and re-layouts  41.2 us (8%)
  matrix products  30.6 us (6%)
  between operations  13.4 us (2%)
    reduce_scatter x1, waiting for transfers between devices, on_device(): lax.psum_scatter(product.reshape(row_count, -1).astype(jnp.bfloat16), 'sl...  430 us
    dot_general x1, matrix products, on_device(): jnp.einsum('tkc,tjc->tkj', v_rows, chosen, preferred_element_type=jnp.flo...  30.6 us
    gather x1, local copies, waits for them, and re-layouts, on_device(): chosen = jnp.take(blocks_held, slot_index, axis=0)  18.5 us
    convert_element_type x1, local copies, waits for them, and re-layouts, on_device(): product.reshape(row_count, -1).astype(jnp.bfloat16)  17.7 us
    all_to_all x1, waiting for transfers between devices, on_device(): lax.all_to_all(outgoing, 'amp', split_axis=1, concat_axis=1, tiled=True)  10.7 us
  transfers between devices with their start and end apart: 2, of which 2 were waited for; matrix products, arithmetic and copies ran while one was open for 0% of the time, Pallas kernels for 0%

commit v1 on v0

v1 whole, which is shorter than its diff:
```python
import functools

import jax
import jax.numpy as jnp
from jax import lax
from jax.experimental import pallas as pl
from jax.experimental.pallas import tpu as pltpu
from jax.sharding import PartitionSpec as P

TB = 128
CHUNKS = 8
EARLY = 2
MESH = pl.DeviceIdType.MESH


def ladder_kernel(
    irrep_ref, t_ref, v_ref, out_ref,
    by_slab, packed, by_amp, stacked, right, v_rows, out_tiles,
    local_sem, tz_send, tz_recv, ta_send, ta_recv, v_send, v_recv, out_sem,
):
    amp_n, slab_n = lax.axis_size("amp"), lax.axis_size("slab")
    amp, slab = lax.axis_index("amp"), lax.axis_index("slab")
    ij = t_ref.shape[1]
    cd = v_ref.shape[1]
    rows_out = out_ref.shape[0]
    chunk = rows_out // CHUNKS
    tiles = irrep_ref.shape[0] // amp_n

    barrier = pltpu.get_barrier_semaphore()

    def greet_slab(k, _):
        pl.semaphore_signal(barrier, inc=1, device_id=(amp, lax.rem(slab + k, slab_n)), device_id_type=MESH)
        return 0

    def greet_amp(k, _):
        pl.semaphore_signal(barrier, inc=1, device_id=(lax.rem(amp + k, amp_n), slab), device_id_type=MESH)
        return 0

    lax.fori_loop(1, slab_n, greet_slab, 0)
    lax.fori_loop(1, amp_n, greet_amp, 0)
    pl.semaphore_wait(barrier, slab_n + amp_n - 2)

    def slab_copy(k):
        return pltpu.make_async_remote_copy(
            src_ref=t_ref, dst_ref=by_slab.at[slab],
            send_sem=tz_send.at[k], recv_sem=tz_recv.at[k],
            device_id=(amp, lax.rem(slab + k, slab_n)), device_id_type=MESH,
        )

    def start_slab(k, _):
        slab_copy(k).start()
        return 0

    lax.fori_loop(1, slab_n, start_slab, 0)
    own_t = pltpu.make_async_copy(t_ref, by_slab.at[slab], local_sem.at[0])
    own_t.start()

    def v_copy(c, k):
        to = lax.rem(slab + k, slab_n)
        return pltpu.make_async_remote_copy(
            src_ref=v_ref.at[pl.ds(pl.multiple_of(to * rows_out + c * chunk, chunk), chunk)],
            dst_ref=v_rows.at[slab, pl.ds(pl.multiple_of(c * chunk, chunk), chunk)],
            send_sem=v_send.at[c, k], recv_sem=v_recv.at[c, k],
            device_id=(amp, to), device_id_type=MESH,
        )

    def start_v(c, _):
        def one(k, _):
            v_copy(c, k).start()
            return 0

        return lax.fori_loop(1, slab_n, one, 0)

    lax.fori_loop(0, EARLY, start_v, 0)
    own_v = pltpu.make_async_copy(
        v_ref.at[pl.ds(pl.multiple_of(slab * rows_out, chunk), rows_out)], v_rows.at[slab], local_sem.at[1]
    )
    own_v.start()

    own_t.wait()

    def await_slab(k, _):
        slab_copy(k).wait()
        return 0

    lax.fori_loop(1, slab_n, await_slab, 0)

    def amp_copy(k):
        return pltpu.make_async_remote_copy(
            src_ref=packed.at[k], dst_ref=by_amp.at[amp],
            send_sem=ta_send.at[k], recv_sem=ta_recv.at[k],
            device_id=(lax.rem(amp + k, amp_n), slab), device_id_type=MESH,
        )

    def pack(k, _):
        to = lax.rem(amp + k, amp_n)
        first, last = irrep_ref[to * tiles], irrep_ref[to * tiles + tiles - 1]

        def one(s, _):
            packed[k, 0, s] = by_slab[s, first]
            packed[k, 1, s] = by_slab[s, last]
            return 0

        lax.fori_loop(0, slab_n, one, 0)
        amp_copy(k).start()
        return 0

    lax.fori_loop(1, amp_n, pack, 0)
    lax.fori_loop(EARLY, CHUNKS, start_v, 0)
    first, last = irrep_ref[amp * tiles], irrep_ref[amp * tiles + tiles - 1]

    def keep(s, _):
        by_amp[amp, 0, s] = by_slab[s, first]
        by_amp[amp, 1, s] = by_slab[s, last]
        return 0

    lax.fori_loop(0, slab_n, keep, 0)
    stacked[...] = jnp.zeros_like(stacked)

    def await_amp(k, _):
        amp_copy(k).wait()
        return 0

    lax.fori_loop(1, amp_n, await_amp, 0)

    def assemble(step, _):
        b, s = step // slab_n, lax.rem(step, slab_n)
        for a in range(amp_n):
            stacked[a * ij:(a + 1) * ij, :] = by_amp[a, b, s].astype(jnp.float32)
        right[b, s] = stacked[...].T.astype(jnp.bfloat16)
        return 0

    lax.fori_loop(0, 2 * slab_n, assemble, 0)
    own_v.wait()

    def out_copy(c):
        place = lax.rem(c, 2)
        return pltpu.make_async_copy(
            out_tiles.at[place], out_ref.at[pl.ds(pl.multiple_of(c * chunk, chunk), chunk)], out_sem.at[place]
        )

    def multiply(c, _):
        def await_v(k, _):
            v_copy(c, k).wait_recv()
            return 0

        lax.fori_loop(1, slab_n, await_v, 0)

        @pl.when(c >= 2)
        def _():
            out_copy(c - 2).wait()

        def tile(i, _):
            at = slab * (rows_out // TB) + c * (chunk // TB) + i
            slot = (irrep_ref[amp * tiles + at] != first).astype(jnp.int32)
            total = jnp.zeros((TB, right.shape[3]), jnp.float32)
            for s in range(slab_n):
                rows = v_rows[s, pl.ds(pl.multiple_of(c * chunk + i * TB, TB), TB)]
                total += jnp.dot(rows, right[slot, s], preferred_element_type=jnp.float32)
            out_tiles[lax.rem(c, 2), pl.ds(pl.multiple_of(i * TB, TB), TB)] = (
                total[:, :out_tiles.shape[2]].astype(jnp.bfloat16)
            )
            return 0

        lax.fori_loop(0, chunk // TB, tile, 0)
        out_copy(c).start()
        return 0

    lax.fori_loop(0, CHUNKS, multiply, 0)
    out_copy(CHUNKS - 2).wait()
    out_copy(CHUNKS - 1).wait()

    def sent(c, _):
        def one(k, _):
            v_copy(c, k).wait_send()
            return 0

        return lax.fori_loop(1, slab_n, one, 0)

    lax.fori_loop(0, CHUNKS, sent, 0)


def on_device(v_slab, t_amp, ab_tile_irrep):
    rows_local, cd = v_slab.shape
    irreps, ij = t_amp.shape[:2]
    amp_n, slab_n = lax.axis_size("amp"), lax.axis_size("slab")
    rows_out = rows_local // slab_n
    ij_all = ij * amp_n
    wide = -(-ij_all // 128) * 128
    any_space = pl.BlockSpec(memory_space=pl.ANY)
    return pl.pallas_call(
        ladder_kernel,
        out_shape=jax.ShapeDtypeStruct((rows_out, ij_all), jnp.bfloat16),
        in_specs=[pl.BlockSpec(memory_space=pltpu.SMEM), any_space, any_space],
        out_specs=any_space,
        scratch_shapes=[
            pltpu.VMEM((slab_n, irreps, ij, cd), jnp.bfloat16),
            pltpu.VMEM((amp_n, 2, slab_n, ij, cd), jnp.bfloat16),
            pltpu.VMEM((amp_n, 2, slab_n, ij, cd), jnp.bfloat16),
            pltpu.VMEM((wide, cd), jnp.float32),
            pltpu.VMEM((2, slab_n, cd, wide), jnp.bfloat16),
            pltpu.VMEM((slab_n, rows_out, cd), jnp.bfloat16),
            pltpu.VMEM((2, rows_out // CHUNKS, ij_all), jnp.bfloat16),
            pltpu.SemaphoreType.DMA((2,)),
            pltpu.SemaphoreType.DMA((slab_n,)),
            pltpu.SemaphoreType.DMA((slab_n,)),
            pltpu.SemaphoreType.DMA((amp_n,)),
            pltpu.SemaphoreType.DMA((amp_n,)),
            pltpu.SemaphoreType.DMA((CHUNKS, slab_n)),
            pltpu.SemaphoreType.DMA((CHUNKS, slab_n)),
            pltpu.SemaphoreType.DMA((2,)),
        ],
        compiler_params=pltpu.CompilerParams(
            collective_id=0, has_side_effects=True, vmem_limit_bytes=48 * 1024 * 1024
        ),
        cost_estimate=pl.CostEstimate(
            flops=2 * rows_out * cd * slab_n * ij_all,
            bytes_accessed=2 * (rows_local * cd + rows_out * ij_all),
            transcendentals=0,
        ),
    )(ab_tile_irrep, t_amp, v_slab)


def solution(mesh):
    placed = (P("amp", "slab"), P(None, "amp", "slab"), P())
    return jax.shard_map(
        on_device, mesh=mesh, in_specs=placed, out_specs=P(("amp", "slab"), None), check_vma=False
    )
```

time: 536 us -> 239 us (0.45)
  waiting for transfers between devices: 441 us -> 0 us
  Pallas kernels: 0 us -> 226 us
  matrix products: 30.6 us -> 0 us
  local copies, waits for them, and re-layouts: 41.2 us -> 12.1 us
  between operations: 13.4 us -> 0.02 us
    reduce_scatter x1 -> x0, waiting for transfers between devices: 430 us -> none  [on_device(): lax.psum_scatter(product.reshape(row_count, -1).astype(jnp.bfloat16), 'sl...]
    pallas_call x0 -> x1, Pallas kernels: none -> 226 us  [on_device(): pl.pallas_call(ladder_kernel, out_shape=jax.ShapeDtypeStruct((rows_out, i...]
    dot_general x1 -> x0, matrix products: 30.6 us -> none  [on_device(): jnp.einsum('tkc,tjc->tkj', v_rows, chosen, preferred_element_type=jnp.flo...]
    gather x2 -> x0, local copies, waits for them, and re-layouts: 21.4 us -> none  [the longest x1 18.5 us: on_device(): chosen = jnp.take(blocks_held, slot_index, axis=0)]
    convert_element_type x1 -> x0, local copies, waits for them, and re-layouts: 17.7 us -> none  [on_device(): product.reshape(row_count, -1).astype(jnp.bfloat16)]
    all_to_all x1 -> x0, waiting for transfers between devices: 10.7 us -> none  [on_device(): lax.all_to_all(outgoing, 'amp', split_axis=1, concat_axis=1, tiled=True)]
    pallas_call x0 -> x1, local copies, waits for them, and re-layouts: none -> 10.4 us  [on_device(): pl.pallas_call(ladder_kernel, out_shape=jax.ShapeDtypeStruct((rows_out, i...]
  transfers between devices with their start and end apart: 2 -> 0, of which waited for: 2 -> 0; matrix products, arithmetic and copies ran while one was open for 0% -> 0% of each run, Pallas kernels for 0% -> 0%
where the time goes in v1:
time: 239 us; the launch traced here: 238 us
  Pallas kernels  226 us (95%)
  local copies, waits for them, and re-layouts  12.1 us (5%)
    pallas_call x1, Pallas kernels, on_device(): pl.pallas_call(ladder_kernel, out_shape=jax.ShapeDtypeStruct((rows_out, i...  226 us
    pallas_call x1, local copies, waits for them, and re-layouts, on_device(): pl.pallas_call(ladder_kernel, out_shape=jax.ShapeDtypeStruct((rows_out, i...  10.4 us

profile of v1, /device:TPU:8, one launch (start us, length us, event | category | flops | bytes accessed | tf_op | source)
XLA Modules:
  0.0 238.1 jit_solution(9262285816452553147)
XLA Ops:
  0.0 1.1 copy.4.t_ref
  1.1 0.0 copy-start
  1.1 0.7 copy-done
  1.8 226.0 %shard_map.37 = bf16[4096,800]{1,0:T(8,128)(2,1)} custom-call(s32[1024]{0:T(1024)S(1)} %copy-done, bf16[8,100,256]{2,1,0:T(8,128)(2,1)S(1)} %copy.4.t_ref, bf16[16384,256]{1,0:T(8,128)(2,1)} %v_ref.1), custom_call_target="tpu_custom_call" | custom-call | flops 6710886400 | bytes 14942208 | tf_op jit(solution)/shard_map/pallas_call | solution.py:191
  227.7 10.4 %copy.5 = bf16[4096,800]{0,1:T(8,128)(2,1)} copy(bf16[4096,800]{1,0:T(8,128)(2,1)} %shard_map.37) | data formatting | bytes 13107200 | tf_op jit(solution)/shard_map/pallas_call | solution.py:191
Async XLA Ops:
  1.1 0.7 copy-start

commit v2 on v1

--- a/solution.py
+++ b/solution.py
@@ -14,17 +14,20 @@
 
 
 def ladder_kernel(
-    irrep_ref, t_ref, v_ref, out_ref,
-    by_slab, packed, by_amp, stacked, right, v_rows, out_tiles,
+    irreps_in, t_ref, v_ref, out_ref,
+    irrep_ref, by_slab, packed, by_amp, stacked, left, v_rows, out_tiles,
     local_sem, tz_send, tz_recv, ta_send, ta_recv, v_send, v_recv, out_sem,
 ):
     amp_n, slab_n = lax.axis_size("amp"), lax.axis_size("slab")
     amp, slab = lax.axis_index("amp"), lax.axis_index("slab")
     ij = t_ref.shape[1]
     cd = v_ref.shape[1]
-    rows_out = out_ref.shape[0]
+    rows_out = out_ref.shape[1]
     chunk = rows_out // CHUNKS
     tiles = irrep_ref.shape[0] // amp_n
+
+    own_irreps = pltpu.make_async_copy(irreps_in, irrep_ref, local_sem.at[2])
+    own_irreps.start()
 
     barrier = pltpu.get_barrier_semaphore()
 
@@ -40,18 +43,27 @@
     lax.fori_loop(1, amp_n, greet_amp, 0)
     pl.semaphore_wait(barrier, slab_n + amp_n - 2)
 
-    def slab_copy(k):
+    def hop(way, r):
+        source = slab - r if way == 0 else slab + r
+        to = slab + 1 if way == 0 else slab - 1
+        held = jnp.clip(source, 0, slab_n - 1)
         return pltpu.make_async_remote_copy(
-            src_ref=t_ref, dst_ref=by_slab.at[slab],
-            send_sem=tz_send.at[k], recv_sem=tz_recv.at[k],
-            device_id=(amp, lax.rem(slab + k, slab_n)), device_id_type=MESH,
-        )
-
-    def start_slab(k, _):
-        slab_copy(k).start()
-        return 0
-
-    lax.fori_loop(1, slab_n, start_slab, 0)
+            src_ref=t_ref if r == 0 else by_slab.at[held], dst_ref=by_slab.at[held],
+            send_sem=tz_send.at[way, r], recv_sem=tz_recv.at[held],
+            device_id=(amp, jnp.clip(to, 0, slab_n - 1)), device_id_type=MESH,
+        )
+
+    def has(way, r):
+        return slab - r >= 0 if way == 0 else slab + r < slab_n
+
+    def passes(way, r):
+        return jnp.logical_and(has(way, r), slab + 1 < slab_n if way == 0 else slab > 0)
+
+    for way in range(2):
+        @pl.when(passes(way, 0))
+        def _():
+            hop(way, 0).start()
+
     own_t = pltpu.make_async_copy(t_ref, by_slab.at[slab], local_sem.at[0])
     own_t.start()
 
@@ -77,13 +89,19 @@
     )
     own_v.start()
 
+    own_irreps.wait()
     own_t.wait()
 
-    def await_slab(k, _):
-        slab_copy(k).wait()
-        return 0
-
-    lax.fori_loop(1, slab_n, await_slab, 0)
+    for r in range(1, slab_n):
+        for way in range(2):
+            @pl.when(has(way, r))
+            def _():
+                hop(way, r).wait_recv()
+
+            if r < slab_n - 1:
+                @pl.when(passes(way, r))
+                def _():
+                    hop(way, r).start()
 
     def amp_copy(k):
         return pltpu.make_async_remote_copy(
@@ -115,7 +133,6 @@
         return 0
 
     lax.fori_loop(0, slab_n, keep, 0)
-    stacked[...] = jnp.zeros_like(stacked)
 
     def await_amp(k, _):
         amp_copy(k).wait()
@@ -127,7 +144,7 @@
         b, s = step // slab_n, lax.rem(step, slab_n)
         for a in range(amp_n):
             stacked[a * ij:(a + 1) * ij, :] = by_amp[a, b, s].astype(jnp.float32)
-        right[b, s] = stacked[...].T.astype(jnp.bfloat16)
+        left[b, s] = stacked[...].astype(jnp.bfloat16)
         return 0
 
     lax.fori_loop(0, 2 * slab_n, assemble, 0)
@@ -136,7 +153,7 @@
     def out_copy(c):
         place = lax.rem(c, 2)
         return pltpu.make_async_copy(
-            out_tiles.at[place], out_ref.at[pl.ds(pl.multiple_of(c * chunk, chunk), chunk)], out_sem.at[place]
+            out_tiles.at[place], out_ref.at[:, pl.ds(pl.multiple_of(c * chunk, chunk), chunk)], out_sem.at[place]
         )
 
     def multiply(c, _):
@@ -153,13 +170,13 @@
         def tile(i, _):
             at = slab * (rows_out // TB) + c * (chunk // TB) + i
             slot = (irrep_ref[amp * tiles + at] != first).astype(jnp.int32)
-            total = jnp.zeros((TB, right.shape[3]), jnp.float32)
+            total = jnp.zeros((left.shape[2], TB), jnp.float32)
             for s in range(slab_n):
                 rows = v_rows[s, pl.ds(pl.multiple_of(c * chunk + i * TB, TB), TB)]
-                total += jnp.dot(rows, right[slot, s], preferred_element_type=jnp.float32)
-            out_tiles[lax.rem(c, 2), pl.ds(pl.multiple_of(i * TB, TB), TB)] = (
-                total[:, :out_tiles.shape[2]].astype(jnp.bfloat16)
-            )
+                total += lax.dot_general(
+                    left[slot, s], rows, (((1,), (1,)), ((), ())), preferred_element_type=jnp.float32
+                )
+            out_tiles[lax.rem(c, 2), :, pl.ds(pl.multiple_of(i * TB, TB), TB)] = total.astype(jnp.bfloat16)
             return 0
 
         lax.fori_loop(0, chunk // TB, tile, 0)
@@ -178,6 +195,11 @@
         return lax.fori_loop(1, slab_n, one, 0)
 
     lax.fori_loop(0, CHUNKS, sent, 0)
+    for r in range(slab_n - 1):
+        for way in range(2):
+            @pl.when(passes(way, r))
+            def _():
+                hop(way, r).wait_send()
 
 
 def on_device(v_slab, t_amp, ab_tile_irrep):
@@ -186,23 +208,23 @@
     amp_n, slab_n = lax.axis_size("amp"), lax.axis_size("slab")
     rows_out = rows_local // slab_n
     ij_all = ij * amp_n
-    wide = -(-ij_all // 128) * 128
     any_space = pl.BlockSpec(memory_space=pl.ANY)
     return pl.pallas_call(
         ladder_kernel,
-        out_shape=jax.ShapeDtypeStruct((rows_out, ij_all), jnp.bfloat16),
-        in_specs=[pl.BlockSpec(memory_space=pltpu.SMEM), any_space, any_space],
+        out_shape=jax.ShapeDtypeStruct((ij_all, rows_out), jnp.bfloat16),
+        in_specs=[any_space] * 3,
         out_specs=any_space,
         scratch_shapes=[
+            pltpu.SMEM(ab_tile_irrep.shape, jnp.int32),
             pltpu.VMEM((slab_n, irreps, ij, cd), jnp.bfloat16),
             pltpu.VMEM((amp_n, 2, slab_n, ij, cd), jnp.bfloat16),
             pltpu.VMEM((amp_n, 2, slab_n, ij, cd), jnp.bfloat16),
-            pltpu.VMEM((wide, cd), jnp.float32),
-            pltpu.VMEM((2, slab_n, cd, wide), jnp.bfloat16),
+            pltpu.VMEM((ij_all, cd), jnp.float32),
+            pltpu.VMEM((2, slab_n, ij_all, cd), jnp.bfloat16),
             pltpu.VMEM((slab_n, rows_out, cd), jnp.bfloat16),
-            pltpu.VMEM((2, rows_out // CHUNKS, ij_all), jnp.bfloat16),
-            pltpu.SemaphoreType.DMA((2,)),
-            pltpu.SemaphoreType.DMA((slab_n,)),
+            pltpu.VMEM((2, ij_all, rows_out // CHUNKS), jnp.bfloat16),
+            pltpu.SemaphoreType.DMA((3,)),
+            pltpu.SemaphoreType.DMA((2, slab_n)),
             pltpu.SemaphoreType.DMA((slab_n,)),
             pltpu.SemaphoreType.DMA((amp_n,)),
             pltpu.SemaphoreType.DMA((amp_n,)),
@@ -218,7 +240,7 @@
             bytes_accessed=2 * (rows_local * cd + rows_out * ij_all),
             transcendentals=0,
         ),
-    )(ab_tile_irrep, t_amp, v_slab)
+    )(ab_tile_irrep, t_amp, v_slab).T
 
 
 def solution(mesh):

time: 239 us -> 218 us (0.912)
  Pallas kernels: 226 us -> 209 us
  local copies, waits for them, and re-layouts: 12.1 us -> 8.25 us
    pallas_call x1, Pallas kernels: 226 us -> 209 us  [on_device(): pl.pallas_call(ladder_kernel, out_shape=jax.ShapeDtypeStruct((ij_all, row...]
    pallas_call x1 -> x0, local copies, waits for them, and re-layouts: 10.4 us -> none  [on_device(): pl.pallas_call(ladder_kernel, out_shape=jax.ShapeDtypeStruct((rows_out, i...]
    unnamed x3 -> x4, local copies, waits for them, and re-layouts: 1.76 us -> 8.25 us
where the time goes in v2:
time: 218 us; the launch traced here: 217 us
  Pallas kernels  209 us (96%)
  local copies, waits for them, and re-layouts  8.25 us (4%)
    pallas_call x1, Pallas kernels, on_device(): pl.pallas_call(ladder_kernel, out_shape=jax.ShapeDtypeStruct((ij_all, row...  209 us
    unnamed x4, local copies, waits for them, and re-layouts  8.25 us

profile of v2, /device:TPU:8, one launch (start us, length us, event | category | flops | bytes accessed | tf_op | source)
XLA Modules:
  0.0 217.3 jit_solution(798941687580663406)
XLA Ops:
  0.0 1.1 copy.4.t_ref
  1.1 0.0 copy-start
  1.1 0.7 copy-done
  1.8 209.0 %shard_map.37 = bf16[800,4096]{1,0:T(8,128)(2,1)} custom-call(s32[1024]{0:T(1024)S(1)} %copy-done, bf16[8,100,256]{2,1,0:T(8,128)(2,1)S(1)} %copy.4.t_ref, bf16[16384,256]{1,0:T(8,128)(2,1)} %v_ref.1), custom_call_target="tpu_custom_call" | custom-call | flops 6710886400 | bytes 14942208 | tf_op jit(solution)/shard_map/pallas_call | solution.py:212
  210.8 6.5 %copy.6 = bf16[4096,800]{0,1:T(8,128)(2,1)} copy(bf16[4096,800]{0,1:T(8,128)(2,1)} %bitcast.1) | data formatting | bytes 13107200
Async XLA Ops:
  1.1 0.7 copy-start

commit v3 on v2

--- a/solution.py
+++ b/solution.py
@@ -8,6 +8,7 @@
 from jax.sharding import PartitionSpec as P
 
 TB = 128
+LANES = 128
 CHUNKS = 8
 EARLY = 2
 MESH = pl.DeviceIdType.MESH
@@ -15,12 +16,12 @@
 
 def ladder_kernel(
     irreps_in, t_ref, v_ref, out_ref,
-    irrep_ref, by_slab, packed, by_amp, stacked, left, v_rows, out_tiles,
-    local_sem, tz_send, tz_recv, ta_send, ta_recv, v_send, v_recv, out_sem,
+    irrep_ref, by_slab, spread, packed, by_amp, stacked, left, v_rows,
+    local_sem, tz_send, tz_recv, ta_send, ta_recv, v_send, v_recv,
 ):
     amp_n, slab_n = lax.axis_size("amp"), lax.axis_size("slab")
     amp, slab = lax.axis_index("amp"), lax.axis_index("slab")
-    ij = t_ref.shape[1]
+    ij, irreps = t_ref.shape[:2]
     cd = v_ref.shape[1]
     rows_out = out_ref.shape[1]
     chunk = rows_out // CHUNKS
@@ -110,13 +111,25 @@
             device_id=(lax.rem(amp + k, amp_n), slab), device_id_type=MESH,
         )
 
+    def widen(s, _):
+        whole = by_slab[s].astype(jnp.float32).reshape(ij * irreps, cd)
+        for q in range(cd // LANES):
+            spread[s, q] = whole[:, q * LANES:(q + 1) * LANES]
+        return 0
+
+    lax.fori_loop(0, slab_n, widen, 0)
+
+    def block_of(s, irrep):
+        parts = [spread[s, q, pl.ds(irrep, ij, irreps), :] for q in range(cd // LANES)]
+        return jnp.concatenate(parts, axis=1).astype(jnp.bfloat16)
+
     def pack(k, _):
         to = lax.rem(amp + k, amp_n)
         first, last = irrep_ref[to * tiles], irrep_ref[to * tiles + tiles - 1]
 
         def one(s, _):
-            packed[k, 0, s] = by_slab[s, first]
-            packed[k, 1, s] = by_slab[s, last]
+            packed[k, 0, s] = block_of(s, first)
+            packed[k, 1, s] = block_of(s, last)
             return 0
 
         lax.fori_loop(0, slab_n, one, 0)
@@ -128,8 +141,8 @@
     first, last = irrep_ref[amp * tiles], irrep_ref[amp * tiles + tiles - 1]
 
     def keep(s, _):
-        by_amp[amp, 0, s] = by_slab[s, first]
-        by_amp[amp, 1, s] = by_slab[s, last]
+        by_amp[amp, 0, s] = block_of(s, first)
+        by_amp[amp, 1, s] = block_of(s, last)
         return 0
 
     lax.fori_loop(0, slab_n, keep, 0)
@@ -150,22 +163,12 @@
     lax.fori_loop(0, 2 * slab_n, assemble, 0)
     own_v.wait()
 
-    def out_copy(c):
-        place = lax.rem(c, 2)
-        return pltpu.make_async_copy(
-            out_tiles.at[place], out_ref.at[:, pl.ds(pl.multiple_of(c * chunk, chunk), chunk)], out_sem.at[place]
-        )
-
     def multiply(c, _):
         def await_v(k, _):
             v_copy(c, k).wait_recv()
             return 0
 
         lax.fori_loop(1, slab_n, await_v, 0)
-
-        @pl.when(c >= 2)
-        def _():
-            out_copy(c - 2).wait()
 
         def tile(i, _):
             at = slab * (rows_out // TB) + c * (chunk // TB) + i
@@ -176,16 +179,13 @@
                 total += lax.dot_general(
                     left[slot, s], rows, (((1,), (1,)), ((), ())), preferred_element_type=jnp.float32
                 )
-            out_tiles[lax.rem(c, 2), :, pl.ds(pl.multiple_of(i * TB, TB), TB)] = total.astype(jnp.bfloat16)
+            out_ref[:, pl.ds(pl.multiple_of(c * chunk + i * TB, TB), TB)] = total.astype(jnp.bfloat16)
             return 0
 
         lax.fori_loop(0, chunk // TB, tile, 0)
-        out_copy(c).start()
         return 0
 
     lax.fori_loop(0, CHUNKS, multiply, 0)
-    out_copy(CHUNKS - 2).wait()
-    out_copy(CHUNKS - 1).wait()
 
     def sent(c, _):
         def one(k, _):
@@ -208,21 +208,21 @@
     amp_n, slab_n = lax.axis_size("amp"), lax.axis_size("slab")
     rows_out = rows_local // slab_n
     ij_all = ij * amp_n
-    any_space = pl.BlockSpec(memory_space=pl.ANY)
+    hbm = pl.BlockSpec(memory_space=pltpu.HBM)
     return pl.pallas_call(
         ladder_kernel,
         out_shape=jax.ShapeDtypeStruct((ij_all, rows_out), jnp.bfloat16),
-        in_specs=[any_space] * 3,
-        out_specs=any_space,
+        in_specs=[hbm] * 3,
+        out_specs=pl.BlockSpec(memory_space=pltpu.VMEM),
         scratch_shapes=[
             pltpu.SMEM(ab_tile_irrep.shape, jnp.int32),
-            pltpu.VMEM((slab_n, irreps, ij, cd), jnp.bfloat16),
+            pltpu.VMEM((slab_n, ij, irreps, cd), jnp.bfloat16),
+            pltpu.VMEM((slab_n, cd // LANES, ij * irreps, LANES), jnp.float32),
             pltpu.VMEM((amp_n, 2, slab_n, ij, cd), jnp.bfloat16),
             pltpu.VMEM((amp_n, 2, slab_n, ij, cd), jnp.bfloat16),
             pltpu.VMEM((ij_all, cd), jnp.float32),
             pltpu.VMEM((2, slab_n, ij_all, cd), jnp.bfloat16),
             pltpu.VMEM((slab_n, rows_out, cd), jnp.bfloat16),
-            pltpu.VMEM((2, ij_all, rows_out // CHUNKS), jnp.bfloat16),
             pltpu.SemaphoreType.DMA((3,)),
             pltpu.SemaphoreType.DMA((2, slab_n)),
             pltpu.SemaphoreType.DMA((slab_n,)),
@@ -230,17 +230,16 @@
             pltpu.SemaphoreType.DMA((amp_n,)),
             pltpu.SemaphoreType.DMA((CHUNKS, slab_n)),
             pltpu.SemaphoreType.DMA((CHUNKS, slab_n)),
-            pltpu.SemaphoreType.DMA((2,)),
         ],
         compiler_params=pltpu.CompilerParams(
-            collective_id=0, has_side_effects=True, vmem_limit_bytes=48 * 1024 * 1024
+            collective_id=0, has_side_effects=True, vmem_limit_bytes=40 * 1024 * 1024
         ),
         cost_estimate=pl.CostEstimate(
             flops=2 * rows_out * cd * slab_n * ij_all,
             bytes_accessed=2 * (rows_local * cd + rows_out * ij_all),
             transcendentals=0,
         ),
-    )(ab_tile_irrep, t_amp, v_slab).T
+    )(*[pltpu.with_memory_space_constraint(x, pltpu.HBM) for x in (ab_tile_irrep, t_amp.transpose(1, 0, 2), v_slab)]).T
 
 
 def solution(mesh):

time: 218 us -> 212 us (0.972)
  local copies, waits for them, and re-layouts: 8.25 us -> 2.79 us
    unnamed x4 -> x1, local copies, waits for them, and re-layouts: 8.25 us -> 2.79 us
where the time goes in v3:
time: 212 us
  Pallas kernels  209 us (99%)
  local copies, waits for them, and re-layouts  2.79 us (1%)
    pallas_call x1, Pallas kernels, on_device(): pl.pallas_call(ladder_kernel, out_shape=jax.ShapeDtypeStruct((ij_all, row...  209 us

profile of v3, /device:TPU:8, one launch (start us, length us, event | category | flops | bytes accessed | tf_op | source)
XLA Modules:
  0.0 212.0 jit_solution(5512414923532837261)
XLA Ops:
  0.0 209.2 %shard_map.37 = bf16[800,4096]{1,0:T(8,128)(2,1)S(1)} custom-call(s32[1024]{0:T(1024)} %irreps_in.1, bf16[100,8,256]{2,1,0:T(8,128)(2,1)} %bitcast.3, bf16[16384,256]{1,0:T(8,128)(2,1)} %v_ref.1), custom_call_target="tpu_custom_call" | custom-call | flops 6710886400 | bytes 14942208 | tf_op jit(solution)/shard_map/pallas_call | solution.py:212
  209.2 2.8 %copy.5 = bf16[4096,800]{0,1:T(8,128)(2,1)} copy(bf16[4096,800]{0,1:T(8,128)(2,1)S(1)} %bitcast.2) | data formatting | bytes 13107200

commit v4 on v3

--- a/solution.py
+++ b/solution.py
@@ -44,26 +44,30 @@
     lax.fori_loop(1, amp_n, greet_amp, 0)
     pl.semaphore_wait(barrier, slab_n + amp_n - 2)
 
-    def hop(way, r):
-        source = slab - r if way == 0 else slab + r
-        to = slab + 1 if way == 0 else slab - 1
-        held = jnp.clip(source, 0, slab_n - 1)
-        return pltpu.make_async_remote_copy(
-            src_ref=t_ref if r == 0 else by_slab.at[held], dst_ref=by_slab.at[held],
-            send_sem=tz_send.at[way, r], recv_sem=tz_recv.at[held],
-            device_id=(amp, jnp.clip(to, 0, slab_n - 1)), device_id_type=MESH,
-        )
-
-    def has(way, r):
-        return slab - r >= 0 if way == 0 else slab + r < slab_n
-
-    def passes(way, r):
-        return jnp.logical_and(has(way, r), slab + 1 < slab_n if way == 0 else slab > 0)
-
-    for way in range(2):
-        @pl.when(passes(way, 0))
+    half = slab_n // 2
+    low = slab < half
+    near_first, far_first = jnp.where(low, 0, half), jnp.where(low, half, 0)
+    far_gate = jnp.where(low, half, half - 1)
+    at_gate = slab == jnp.where(low, half - 1, half)
+
+    def own_copy(to):
+        return pltpu.make_async_remote_copy(
+            src_ref=t_ref, dst_ref=by_slab.at[slab], send_sem=tz_send.at[slab, to], recv_sem=tz_recv.at[slab],
+            device_id=(amp, to), device_id_type=MESH,
+        )
+
+    def far_copy(source, to):
+        return pltpu.make_async_remote_copy(
+            src_ref=by_slab.at[source], dst_ref=by_slab.at[source],
+            send_sem=tz_send.at[source, to], recv_sem=tz_recv.at[source],
+            device_id=(amp, to), device_id_type=MESH,
+        )
+
+    own_copy(far_gate).start()
+    for i in range(half):
+        @pl.when(near_first + i != slab)
         def _():
-            hop(way, 0).start()
+            own_copy(near_first + i).start()
 
     own_t = pltpu.make_async_copy(t_ref, by_slab.at[slab], local_sem.at[0])
     own_t.start()
@@ -93,16 +97,17 @@
     own_irreps.wait()
     own_t.wait()
 
-    for r in range(1, slab_n):
-        for way in range(2):
-            @pl.when(has(way, r))
+    for i in range(half):
+        far_copy(far_first + i, far_gate).wait_recv()
+        for j in range(half):
+            @pl.when(jnp.logical_and(at_gate, near_first + j != slab))
             def _():
-                hop(way, r).wait_recv()
-
-            if r < slab_n - 1:
-                @pl.when(passes(way, r))
-                def _():
-                    hop(way, r).start()
+                far_copy(far_first + i, near_first + j).start()
+
+    for i in range(half):
+        @pl.when(near_first + i != slab)
+        def _():
+            far_copy(near_first + i, far_gate).wait_recv()
 
     def amp_copy(k):
         return pltpu.make_async_remote_copy(
@@ -195,11 +200,16 @@
         return lax.fori_loop(1, slab_n, one, 0)
 
     lax.fori_loop(0, CHUNKS, sent, 0)
-    for r in range(slab_n - 1):
-        for way in range(2):
-            @pl.when(passes(way, r))
+    own_copy(far_gate).wait_send()
+    for i in range(half):
+        @pl.when(near_first + i != slab)
+        def _():
+            own_copy(near_first + i).wait_send()
+
+        for j in range(half):
+            @pl.when(jnp.logical_and(at_gate, near_first + j != slab))
             def _():
-                hop(way, r).wait_send()
+                far_copy(far_first + i, near_first + j).wait_send()
 
 
 def on_device(v_slab, t_amp, ab_tile_irrep):
@@ -224,7 +234,7 @@
             pltpu.VMEM((2, slab_n, ij_all, cd), jnp.bfloat16),
             pltpu.VMEM((slab_n, rows_out, cd), jnp.bfloat16),
             pltpu.SemaphoreType.DMA((3,)),
-            pltpu.SemaphoreType.DMA((2, slab_n)),
+            pltpu.SemaphoreType.DMA((slab_n, slab_n)),
             pltpu.SemaphoreType.DMA((slab_n,)),
             pltpu.SemaphoreType.DMA((amp_n,)),
             pltpu.SemaphoreType.DMA((amp_n,)),

time: 212 us -> 209 us (0.986)
  Pallas kernels: 209 us -> 206 us
    pallas_call x1, Pallas kernels: 209 us -> 206 us  [on_device(): pl.pallas_call(ladder_kernel, out_shape=jax.ShapeDtypeStruct((ij_all, row...]
where the time goes in v4:
time: 209 us
  Pallas kernels  206 us (99%)
  local copies, waits for them, and re-layouts  2.79 us (1%)
    pallas_call x1, Pallas kernels, on_device(): pl.pallas_call(ladder_kernel, out_shape=jax.ShapeDtypeStruct((ij_all, row...  206 us

profile of v4, /device:TPU:8, one launch (start us, length us, event | category | flops | bytes accessed | tf_op | source)
XLA Modules:
  0.0 209.0 jit_solution(14559768553775379734)
XLA Ops:
  0.0 206.2 %shard_map.37 = bf16[800,4096]{1,0:T(8,128)(2,1)S(1)} custom-call(s32[1024]{0:T(1024)} %irreps_in.1, bf16[100,8,256]{2,1,0:T(8,128)(2,1)} %bitcast.3, bf16[16384,256]{1,0:T(8,128)(2,1)} %v_ref.1), custom_call_target="tpu_custom_call" | custom-call | flops 6710886400 | bytes 14942208 | tf_op jit(solution)/shard_map/pallas_call | solution.py:222
  206.3 2.8 %copy.5 = bf16[4096,800]{0,1:T(8,128)(2,1)} copy(bf16[4096,800]{0,1:T(8,128)(2,1)S(1)} %bitcast.2) | data formatting | bytes 13107200

commit v5 on v4

--- a/solution.py
+++ b/solution.py
@@ -9,8 +9,9 @@
 
 TB = 128
 LANES = 128
-CHUNKS = 8
+CHUNK = 4 * TB
 EARLY = 2
+AHEAD = 2
 MESH = pl.DeviceIdType.MESH
 
 
@@ -24,7 +25,9 @@
     ij, irreps = t_ref.shape[:2]
     cd = v_ref.shape[1]
     rows_out = out_ref.shape[1]
-    chunk = rows_out // CHUNKS
+    long_n = rows_out // CHUNK - 1
+    short_n = CHUNK // TB
+    chunks = long_n + short_n
     tiles = irrep_ref.shape[0] // amp_n
 
     own_irreps = pltpu.make_async_copy(irreps_in, irrep_ref, local_sem.at[2])
@@ -72,25 +75,35 @@
     own_t = pltpu.make_async_copy(t_ref, by_slab.at[slab], local_sem.at[0])
     own_t.start()
 
-    def v_copy(c, k):
+    def place(c, size):
+        if size == CHUNK:
+            return pl.multiple_of(c * CHUNK, CHUNK)
+        return pl.multiple_of(long_n * CHUNK + (c - long_n) * TB, TB)
+
+    def v_copy(c, k, size):
         to = lax.rem(slab + k, slab_n)
-        return pltpu.make_async_remote_copy(
-            src_ref=v_ref.at[pl.ds(pl.multiple_of(to * rows_out + c * chunk, chunk), chunk)],
-            dst_ref=v_rows.at[slab, pl.ds(pl.multiple_of(c * chunk, chunk), chunk)],
+        row = place(c, size)
+        return pltpu.make_async_remote_copy(
+            src_ref=v_ref.at[pl.ds(pl.multiple_of(to * rows_out + row, TB), size)],
+            dst_ref=v_rows.at[slab, pl.ds(row, size)],
             send_sem=v_send.at[c, k], recv_sem=v_recv.at[c, k],
             device_id=(amp, to), device_id_type=MESH,
         )
 
-    def start_v(c, _):
-        def one(k, _):
-            v_copy(c, k).start()
-            return 0
-
-        return lax.fori_loop(1, slab_n, one, 0)
-
-    lax.fori_loop(0, EARLY, start_v, 0)
+    def start_v(size):
+        def start(c, _):
+            def one(k, _):
+                v_copy(c, k, size).start()
+                return 0
+
+            return lax.fori_loop(1, slab_n, one, 0)
+
+        return start
+
+    early = min(EARLY, long_n)
+    lax.fori_loop(0, early, start_v(CHUNK), 0)
     own_v = pltpu.make_async_copy(
-        v_ref.at[pl.ds(pl.multiple_of(slab * rows_out, chunk), rows_out)], v_rows.at[slab], local_sem.at[1]
+        v_ref.at[pl.ds(pl.multiple_of(slab * rows_out, TB), rows_out)], v_rows.at[slab], local_sem.at[1]
     )
     own_v.start()
 
@@ -142,7 +155,8 @@
         return 0
 
     lax.fori_loop(1, amp_n, pack, 0)
-    lax.fori_loop(EARLY, CHUNKS, start_v, 0)
+    lax.fori_loop(early, long_n, start_v(CHUNK), 0)
+    lax.fori_loop(long_n, long_n + AHEAD, start_v(TB), 0)
     first, last = irrep_ref[amp * tiles], irrep_ref[amp * tiles + tiles - 1]
 
     def keep(s, _):
@@ -168,38 +182,52 @@
     lax.fori_loop(0, 2 * slab_n, assemble, 0)
     own_v.wait()
 
-    def multiply(c, _):
-        def await_v(k, _):
-            v_copy(c, k).wait_recv()
-            return 0
-
-        lax.fori_loop(1, slab_n, await_v, 0)
-
-        def tile(i, _):
-            at = slab * (rows_out // TB) + c * (chunk // TB) + i
-            slot = (irrep_ref[amp * tiles + at] != first).astype(jnp.int32)
-            total = jnp.zeros((left.shape[2], TB), jnp.float32)
-            for s in range(slab_n):
-                rows = v_rows[s, pl.ds(pl.multiple_of(c * chunk + i * TB, TB), TB)]
-                total += lax.dot_general(
-                    left[slot, s], rows, (((1,), (1,)), ((), ())), preferred_element_type=jnp.float32
-                )
-            out_ref[:, pl.ds(pl.multiple_of(c * chunk + i * TB, TB), TB)] = total.astype(jnp.bfloat16)
-            return 0
-
-        lax.fori_loop(0, chunk // TB, tile, 0)
-        return 0
-
-    lax.fori_loop(0, CHUNKS, multiply, 0)
-
-    def sent(c, _):
-        def one(k, _):
-            v_copy(c, k).wait_send()
-            return 0
-
-        return lax.fori_loop(1, slab_n, one, 0)
-
-    lax.fori_loop(0, CHUNKS, sent, 0)
+    def multiply(size):
+        def step(c, _):
+            def await_v(k, _):
+                v_copy(c, k, size).wait_recv()
+                return 0
+
+            lax.fori_loop(1, slab_n, await_v, 0)
+            if size == TB:
+                @pl.when(c + AHEAD < chunks)
+                def _():
+                    start_v(TB)(c + AHEAD, 0)
+
+            row = place(c, size)
+
+            def tile(i, _):
+                at = pl.multiple_of(row + i * TB, TB)
+                held = amp * tiles + slab * (rows_out // TB) + at // TB
+                slot = (irrep_ref[held] != first).astype(jnp.int32)
+                total = jnp.zeros((left.shape[2], TB), jnp.float32)
+                for s in range(slab_n):
+                    total += lax.dot_general(
+                        left[slot, s], v_rows[s, pl.ds(at, TB)], (((1,), (1,)), ((), ())),
+                        preferred_element_type=jnp.float32,
+                    )
+                out_ref[:, pl.ds(at, TB)] = total.astype(jnp.bfloat16)
+                return 0
+
+            return lax.fori_loop(0, size // TB, tile, 0)
+
+        return step
+
+    lax.fori_loop(0, long_n, multiply(CHUNK), 0)
+    lax.fori_loop(long_n, chunks, multiply(TB), 0)
+
+    def sent(size):
+        def step(c, _):
+            def one(k, _):
+                v_copy(c, k, size).wait_send()
+                return 0
+
+            return lax.fori_loop(1, slab_n, one, 0)
+
+        return step
+
+    lax.fori_loop(0, long_n, sent(CHUNK), 0)
+    lax.fori_loop(long_n, chunks, sent(TB), 0)
     own_copy(far_gate).wait_send()
     for i in range(half):
         @pl.when(near_first + i != slab)
@@ -218,6 +246,7 @@
     amp_n, slab_n = lax.axis_size("amp"), lax.axis_size("slab")
     rows_out = rows_local // slab_n
     ij_all = ij * amp_n
+    chunks = rows_out // CHUNK - 1 + CHUNK // TB
     hbm = pl.BlockSpec(memory_space=pltpu.HBM)
     return pl.pallas_call(
         ladder_kernel,
@@ -238,8 +267,8 @@
             pltpu.SemaphoreType.DMA((slab_n,)),
             pltpu.SemaphoreType.DMA((amp_n,)),
             pltpu.SemaphoreType.DMA((amp_n,)),
-            pltpu.SemaphoreType.DMA((CHUNKS, slab_n)),
-            pltpu.SemaphoreType.DMA((CHUNKS, slab_n)),
+            pltpu.SemaphoreType.DMA((chunks, slab_n)),
+            pltpu.SemaphoreType.DMA((chunks, slab_n)),
         ],
         compiler_params=pltpu.CompilerParams(
             collective_id=0, has_side_effects=True, vmem_limit_bytes=40 * 1024 * 1024

time: 209 us -> 209 us (level)
  no operation moved by 1% of the time
where the time goes in v5:
time: 209 us; the launch traced here: 208 us
  Pallas kernels  205 us (98%)
  local copies, waits for them, and re-layouts  2.79 us (1%)
    pallas_call x1, Pallas kernels, on_device(): pl.pallas_call(ladder_kernel, out_shape=jax.ShapeDtypeStruct((ij_all, row...  205 us

profile of v5, /device:TPU:8, one launch (start us, length us, event | category | flops | bytes accessed | tf_op | source)
XLA Modules:
  0.0 207.5 jit_solution(5812559667930484160)
XLA Ops:
  0.0 204.7 %shard_map.37 = bf16[800,4096]{1,0:T(8,128)(2,1)S(1)} custom-call(s32[1024]{0:T(1024)} %irreps_in.1, bf16[100,8,256]{2,1,0:T(8,128)(2,1)} %bitcast.3, bf16[16384,256]{1,0:T(8,128)(2,1)} %v_ref.1), custom_call_target="tpu_custom_call" | custom-call | flops 6710886400 | bytes 14942208 | tf_op jit(solution)/shard_map/pallas_call | solution.py:251
  204.7 2.8 %copy.5 = bf16[4096,800]{0,1:T(8,128)(2,1)} copy(bf16[4096,800]{0,1:T(8,128)(2,1)S(1)} %bitcast.2) | data formatting | bytes 13107200
